TPU v7x, 32 devices: a whole 2x2x4 slice. The times are simulated.
32 devices in a mesh: dp: 4 (over z), node: 8 (over y, x, core).
Axes of the slice: x: 2, y: 2, z: 4, core: 2. Of those that a mesh axis runs over, the one named last changes fastest.
Arguments:
- vertex_embeddings: bfloat16 [4, 4096, 768], P('dp', 'node'), may hold values from -12 to 12
- incoming_adjoint: bfloat16 [4, 4096, 768], P('dp', 'node'), may hold values from -6 to 6
- asking_projector_matrix: bfloat16 [768, 768], replicated, may hold values from -0.21875 to 0.21875
- lookup_projector_matrix: bfloat16 [768, 768], replicated, may hold values from -0.21875 to 0.21875
- content_projector_matrix: bfloat16 [768, 768], replicated, may hold values from -0.21875 to 0.21875
- final_projector_matrix: bfloat16 [768, 768], replicated, may hold values from -0.21875 to 0.21875
- grouped_vertex_permutation: int32 [4, 4096], P('dp'), may hold values from 0 to 4095, as said below
- listed_tiles: int32 [4, 32, 32, 4], P('dp'), may hold values from 0 to 31, as said below
- active_tile_tally: int32 [4, 32, 32], P('dp'), may hold values from 1 to 4, as said below
Outputs:
- sublayer_yield: bfloat16 [4, 4096, 768], P('dp', 'node')
- embedding_derivative: bfloat16 [4, 4096, 768], P('dp', 'node')
- grad_query: float32 [768, 768], replicated
- grad_key: float32 [768, 768], replicated
- grad_value: float32 [768, 768], replicated
- grad_out: float32 [768, 768], replicated
Inputs may be any that keep to these rules, and one draw needn't show every extreme that they name: `grouped_vertex_permutation`: each subgraph's row is a permutation of the 4096 nodes. listed_tiles[g, h, b, :] are 4 distinct key block numbers, the first of them b. `active_tile_tally`: for every subgraph and head some query block has 4.
All inputs are finite; a program needn't handle non-finite values.
Results may differ from a plain program's by a relative error of at most 0.015.
The roundings to bfloat16 on the way count: a program that leaves them out, or rounds other values in their place, can miss the bound.
Values may be sent and summed in bfloat16 or wider, within the bound.
A program may use at most 128 MiB of HBM per device.

v0:
```python
import math

import jax
import jax.numpy as jnp
from jax import lax
from jax.sharding import PartitionSpec as P

H = 32
HD = 24
BLOCK = 128


def project(weight, rows):
    return lax.dot_general(
        weight, rows, (((0,), (1,)), ((), ())), preferred_element_type=jnp.float32
    ).astype(jnp.bfloat16)


def local(
    vertex_embeddings,
    incoming_adjoint,
    asking_projector_matrix,
    lookup_projector_matrix,
    content_projector_matrix,
    final_projector_matrix,
    grouped_vertex_permutation,
    listed_tiles,
    active_tile_tally,
):
    rows = vertex_embeddings[0]
    cotan = incoming_adjoint[0]
    parts = lax.axis_size("node")
    local_heads = H // parts
    score_scale = 1.0 / math.sqrt(HD)
    pq = project(asking_projector_matrix, rows)
    pk = project(lookup_projector_matrix, rows)
    pv = project(content_projector_matrix, rows)
    upstream = lax.dot_general(
        final_projector_matrix, cotan, (((1,), (1,)), ((), ())), preferred_element_type=jnp.float32
    ).astype(jnp.bfloat16)
    qkv_heads = lax.all_to_all(
        jnp.stack([pq, pk, pv]), "node", split_axis=1, concat_axis=2, tiled=True
    )
    up_heads = lax.all_to_all(upstream, "node", split_axis=0, concat_axis=1, tiled=True)
    order = grouped_vertex_permutation[0]
    total = order.shape[0]
    nblocks = total // BLOCK
    neighbor_slots = listed_tiles.shape[-1]

    def to_blocks(arr):
        arr = jnp.take(arr, order, axis=-1)
        return arr.reshape(arr.shape[:-2] + (local_heads, HD, nblocks, BLOCK))

    blocked = to_blocks(qkv_heads)
    queries = blocked[0]
    keys = blocked[1].transpose(0, 2, 1, 3)
    values = blocked[2].transpose(0, 2, 1, 3)
    up_blocked = to_blocks(up_heads)
    first = lax.axis_index("node") * local_heads
    lists = lax.dynamic_slice_in_dim(listed_tiles[0], first, local_heads, 0)
    live_counts = lax.dynamic_slice_in_dim(active_tile_tally[0], first, local_heads, 0)
    group = 8
    turns = nblocks // group
    pick = jax.vmap(lambda table, where: table[where])
    accumulate = jax.vmap(lambda acc, where, vals: acc.at[where].add(vals))

    def step(carry, turn):
        dk_acc, dv_acc = carry
        start = turn * group
        q_part = lax.dynamic_slice_in_dim(queries, start, group, 2)
        up_part = lax.dynamic_slice_in_dim(up_blocked, start, group, 2)
        ids = lax.dynamic_slice_in_dim(lists, start, group, 1)
        live_now = lax.dynamic_slice_in_dim(live_counts, start, group, 1)
        k_got = pick(keys, ids)
        v_got = pick(values, ids)
        score = (
            jnp.einsum("hdgi,hgmdj->hgimj", q_part, k_got, preferred_element_type=jnp.float32)
            * score_scale
        )
        live = (jnp.arange(neighbor_slots)[None, None, :] < live_now[:, :, None])[
            :, :, None, :, None
        ]
        score = jnp.where(live, score, -1e30)
        top = jnp.max(score, axis=(3, 4), keepdims=True)
        expo = jnp.exp(score - top)
        prob = expo / jnp.sum(expo, axis=(3, 4), keepdims=True)
        probability_block = prob.astype(jnp.bfloat16)
        output_rows = jnp.einsum(
            "hgimj,hgmdj->hdgi", probability_block, v_got, preferred_element_type=jnp.float32
        ).astype(jnp.bfloat16)
        probability_gradient = jnp.einsum(
            "hdgi,hgmdj->hgimj", up_part, v_got, preferred_element_type=jnp.float32
        )
        delta = jnp.sum(prob * probability_gradient, axis=(3, 4), keepdims=True)
        score_gradient = (prob * (probability_gradient - delta) * score_scale).astype(jnp.bfloat16)
        query_gradient = jnp.einsum(
            "hgimj,hgmdj->hdgi", score_gradient, k_got, preferred_element_type=jnp.float32
        )
        dk_got = jnp.einsum(
            "hgimj,hdgi->hgmdj", score_gradient, q_part, preferred_element_type=jnp.float32
        )
        dv_got = jnp.einsum(
            "hgimj,hdgi->hgmdj", probability_block, up_part, preferred_element_type=jnp.float32
        )
        flat_ids = ids.reshape(local_heads, group * neighbor_slots)
        dk_acc = accumulate(
            dk_acc, flat_ids, dk_got.reshape(local_heads, group * neighbor_slots, HD, BLOCK)
        )
        dv_acc = accumulate(
            dv_acc, flat_ids, dv_got.reshape(local_heads, group * neighbor_slots, HD, BLOCK)
        )
        return ((dk_acc, dv_acc), (output_rows, query_gradient))

    zeros = jnp.zeros((local_heads, nblocks, HD, BLOCK), jnp.float32)
    (dk_acc, dv_acc), (out_steps, dq_steps) = lax.scan(step, (zeros, zeros), jnp.arange(turns))
    feats = local_heads * HD

    def from_steps(arr):
        return arr.transpose(1, 2, 0, 3, 4).reshape(feats, total)

    def from_acc(arr):
        return arr.transpose(0, 2, 1, 3).reshape(feats, total)

    def restore(arr):
        return jnp.zeros_like(arr).at[:, order].set(arr)

    out_heads = restore(from_steps(out_steps))
    dq_heads = restore(from_steps(dq_steps)).astype(jnp.bfloat16)
    dk_heads = restore(from_acc(dk_acc)).astype(jnp.bfloat16)
    dv_heads = restore(from_acc(dv_acc)).astype(jnp.bfloat16)
    out_nodes = lax.all_to_all(out_heads, "node", split_axis=1, concat_axis=0, tiled=True)
    grads_nodes = lax.all_to_all(
        jnp.stack([dq_heads, dk_heads, dv_heads]), "node", split_axis=2, concat_axis=1, tiled=True
    )
    dims_first = (((0,), (0,)), ((), ()))
    result = lax.dot_general(
        out_nodes, final_projector_matrix, dims_first, preferred_element_type=jnp.float32
    ).astype(jnp.bfloat16)
    dims_back = (((0,), (1,)), ((), ()))
    backward = (
        lax.dot_general(
            grads_nodes[0], asking_projector_matrix, dims_back, preferred_element_type=jnp.float32
        )
        + lax.dot_general(
            grads_nodes[1], lookup_projector_matrix, dims_back, preferred_element_type=jnp.float32
        )
        + lax.dot_general(
            grads_nodes[2], content_projector_matrix, dims_back, preferred_element_type=jnp.float32
        )
    ).astype(jnp.bfloat16)
    dims_weight = (((0,), (1,)), ((), ()))
    stacked = jnp.stack(
        [
            lax.dot_general(rows, grads_nodes[0], dims_weight, preferred_element_type=jnp.float32),
            lax.dot_general(rows, grads_nodes[1], dims_weight, preferred_element_type=jnp.float32),
            lax.dot_general(rows, grads_nodes[2], dims_weight, preferred_element_type=jnp.float32),
            jnp.dot(out_nodes, cotan, preferred_element_type=jnp.float32),
        ]
    )
    share = lax.psum_scatter(
        stacked.astype(jnp.bfloat16), "node", scatter_dimension=1, tiled=True
    ).astype(jnp.float32)
    share = lax.psum(share.astype(jnp.bfloat16), "dp").astype(jnp.float32)
    summed = lax.all_gather(share.astype(jnp.bfloat16), "node", axis=1, tiled=True).astype(
        share.dtype
    )
    factor = 1.0 / math.sqrt(lax.axis_size("dp") * total)
    summed = summed * factor
    return (result[None], backward[None], summed[0], summed[1], summed[2], summed[3])


def solution(mesh):
    placed = (
        P("dp", "node", None),
        P("dp", "node", None),
        P(),
        P(),
        P(),
        P(),
        P("dp", None),
        P("dp", None, None, None),
        P("dp", None, None),
    )
    return jax.shard_map(
        local,
        mesh=mesh,
        in_specs=placed,
        out_specs=(P("dp", "node", None), P("dp", "node", None), P(), P(), P(), P()),
        check_vma=False,
    )
```

profile of v0, /device:TPU:0, one launch (start us, length us, event | category | flops | bytes accessed | tf_op | source)
XLA Modules:
  0.0 833.8 jit_solution(350163024695273675)
XLA Ops:
  37.6 12.1 %gather_fusion.3 = bf16[4096,96]{1,0:T(8,128)(2,1)S(1)} fusion(bf16[96,4096]{0,1:T(8,128)(2,1)S(1)} %bitcast.267, s32[4096]{0:T(1024)S(1)} %broadcast_clamp_fusion), kind=kCustom, calls=%fused_computation.3 | custom fusion | bytes 1589248 | tf_op jit(solution)/shard_map/jit(_take)/gather | solution.py:51
  51.5 20.1 %all-to-all-done = bf16[3,768,512]{2,0,1:T(4,128)(2,1)} async-done(((bf16[3,768,512]{2,0,1:T(4,128)(2,1)}), bf16[3,768,512]{2,0,1:T(4,128)(2,1)}, u32[]{:S(2)}, u32[]{:S(2)}) %all-to-all-start) | async-done | bytes 2359328 | tf_op jit(solution)/shard_map/all_to_all | solution.py:41
  79.2 30.7 %gather_fusion.2 = bf16[4096,3,96]{2,1,0:T(4,128)(2,1)} fusion(bf16[3,96,4096]{1,0,2:T(4,128)(2,1)} %bitcast.271, s32[4096]{0:T(1024)S(1)} %broadcast_clamp_fusion), kind=kCustom, calls=%fused_computation.2 | custom fusion | bytes 4734976 | tf_op jit(solution)/shard_map/jit(_take)/gather | solution.py:51
  109.9 16.5 %select_bitcast_fusion = bf16[3,96,4096]{1,0,2:T(4,128)(2,1)S(1)} fusion(bf16[4096,3,96]{2,1,0:T(4,128)(2,1)} %gather_fusion.2, pred[4096]{0:T(1024)(128)(4,1)S(1)} %copy-done.22), kind=kLoop, calls=%fused_computation.53 | loop fusion | flops 1179648 | bytes 4722688 | tf_op jit(solution)/shard_map/jit(_take)/select_n | solution.py:51
  155.2 297.2 %while.16 = (s32[]{:T(128)}, f32[4,32,24,128]{3,2,1,0:T(8,128)}, f32[4,32,24,128]{3,2,1,0:T(8,128)S(1)}, bf16[4,4,24,8,128]{4,2,3,1,0:T(8,128)(2,1)}, f32[4,4,24...) while((s32[]{:T(128)}, f32[4,32,24,128]{3,2,1,0:T(8,128)}, ...), condition=%wide.region_6.7_spmd, body=%wide.region_0.6_spmd.sunk | while | flops 669866624 | bytes 200112496 | solution.py:115
  171.7 6.5 fusion.115
  183.3 11.7 %scatter_fusion.1 = f32[4,32,24,128]{3,2,1,0:T(8,128)S(1)} fusion(f32[4,32,24,128]{3,2,1,0:T(8,128)S(1)} %get-tuple-element.274, s32[128]{0:T(128)S(1)} %reshape.248, f32[128,24,128]{2,1,0:T(8,128)} %bitcast.268), kind=kCustom, calls=%fused_computation.5.clone.1 | custom fusion | flops 393216 | bytes 4719616 | tf_op jit(solution)/shard_map/while/body/eval_jaxpr/vmap()/scatter-add | solution.py:65
  195.0 7.2 multiply_reduce_fusion.2
  210.5 15.5 %scatter_fusion = f32[4,32,24,128]{3,2,1,0:T(8,128)} fusion(f32[4,32,24,128]{3,2,1,0:T(8,128)} %get-tuple-element.273, s32[128]{0:T(128)S(1)} %reshape.248, f32[128,24,128]{2,1,0:T(8,128)S(1)} %bitcast.264), kind=kCustom, calls=%fused_computation.4.clone.1 | custom fusion | flops 393216 | bytes 4719616 | tf_op jit(solution)/shard_map/while/body/eval_jaxpr/vmap()/scatter-add | solution.py:65
  245.8 6.5 fusion.115
  257.5 11.7 %scatter_fusion.1 = f32[4,32,24,128]{3,2,1,0:T(8,128)S(1)} fusion(f32[4,32,24,128]{3,2,1,0:T(8,128)S(1)} %get-tuple-element.274, s32[128]{0:T(128)S(1)} %reshape.248, f32[128,24,128]{2,1,0:T(8,128)} %bitcast.268), kind=kCustom, calls=%fused_computation.5.clone.1 | custom fusion | flops 393216 | bytes 4719616 | tf_op jit(solution)/shard_map/while/body/eval_jaxpr/vmap()/scatter-add | solution.py:65
  269.2 7.2 multiply_reduce_fusion.2
  284.7 15.5 %scatter_fusion = f32[4,32,24,128]{3,2,1,0:T(8,128)} fusion(f32[4,32,24,128]{3,2,1,0:T(8,128)} %get-tuple-element.273, s32[128]{0:T(128)S(1)} %reshape.248, f32[128,24,128]{2,1,0:T(8,128)S(1)} %bitcast.264), kind=kCustom, calls=%fused_computation.4.clone.1 | custom fusion | flops 393216 | bytes 4719616 | tf_op jit(solution)/shard_map/while/body/eval_jaxpr/vmap()/scatter-add | solution.py:65
  320.0 6.5 fusion.115
  331.6 11.7 %scatter_fusion.1 = f32[4,32,24,128]{3,2,1,0:T(8,128)S(1)} fusion(f32[4,32,24,128]{3,2,1,0:T(8,128)S(1)} %get-tuple-element.274, s32[128]{0:T(128)S(1)} %reshape.248, f32[128,24,128]{2,1,0:T(8,128)} %bitcast.268), kind=kCustom, calls=%fused_computation.5.clone.1 | custom fusion | flops 393216 | bytes 4719616 | tf_op jit(solution)/shard_map/while/body/eval_jaxpr/vmap()/scatter-add | solution.py:65
  343.3 7.2 multiply_reduce_fusion.2
  358.8 15.5 %scatter_fusion = f32[4,32,24,128]{3,2,1,0:T(8,128)} fusion(f32[4,32,24,128]{3,2,1,0:T(8,128)} %get-tuple-element.273, s32[128]{0:T(128)S(1)} %reshape.248, f32[128,24,128]{2,1,0:T(8,128)S(1)} %bitcast.264), kind=kCustom, calls=%fused_computation.4.clone.1 | custom fusion | flops 393216 | bytes 4719616 | tf_op jit(solution)/shard_map/while/body/eval_jaxpr/vmap()/scatter-add | solution.py:65
  405.8 11.6 %scatter_fusion.1 = f32[4,32,24,128]{3,2,1,0:T(8,128)S(1)} fusion(f32[4,32,24,128]{3,2,1,0:T(8,128)S(1)} %get-tuple-element.274, s32[128]{0:T(128)S(1)} %reshape.248, f32[128,24,128]{2,1,0:T(8,128)} %bitcast.268), kind=kCustom, calls=%fused_computation.5.clone.1 | custom fusion | flops 393216 | bytes 4719616 | tf_op jit(solution)/shard_map/while/body/eval_jaxpr/vmap()/scatter-add | solution.py:65
  417.5 7.2 multiply_reduce_fusion.2
  433.0 15.5 %scatter_fusion = f32[4,32,24,128]{3,2,1,0:T(8,128)} fusion(f32[4,32,24,128]{3,2,1,0:T(8,128)} %get-tuple-element.273, s32[128]{0:T(128)S(1)} %reshape.248, f32[128,24,128]{2,1,0:T(8,128)S(1)} %bitcast.264), kind=kCustom, calls=%fused_computation.4.clone.1 | custom fusion | flops 393216 | bytes 4719616 | tf_op jit(solution)/shard_map/while/body/eval_jaxpr/vmap()/scatter-add | solution.py:65
  469.5 11.3 %scatter_custom_fusion.2 = bf16[96,4096]{0,1:T(8,128)(2,1)S(1)} fusion(s32[4096]{0:T(1024)} %bitcast.306, bf16[4096,96]{1,0:T(8,128)(2,1)S(1)} %copy.109, bf16[]{:T(256)} %constant.39.clone.1), kind=kCustom, calls=%fused_computation.102 | custom fusion | bytes 786944 | tf_op jit(solution)/shard_map/scatter | solution.py:125
  486.2 11.4 %scatter_custom_fusion.4 = f32[96,4096]{0,1:T(8,128)S(1)} fusion(s32[4096]{0:T(1024)} %bitcast.307, f32[4096,96]{1,0:T(8,128)} %copy.114, f32[]{:T(128)} %constant.42.clone.1), kind=kCustom, calls=%fused_computation.87 | custom fusion | bytes 1573376 | tf_op jit(solution)/shard_map/scatter | solution.py:125
  497.6 12.3 %scatter_custom_fusion.5 = f32[96,4096]{0,1:T(8,128)} fusion(s32[4096]{0:T(1024)} %bitcast.308, f32[4096,96]{1,0:T(8,128)} %copy.116, f32[]{:T(128)} %constant.42.clone.1), kind=kCustom, calls=%fused_computation.85 | custom fusion | bytes 1573376 | tf_op jit(solution)/shard_map/scatter | solution.py:125
  513.1 11.6 %scatter_custom_fusion.3 = f32[96,4096]{0,1:T(8,128)S(1)} fusion(s32[4096]{0:T(1024)} %bitcast.309, f32[4096,96]{1,0:T(8,128)} %copy.112, f32[]{:T(128)} %constant.42.clone.1), kind=kCustom, calls=%fused_computation.89 | custom fusion | bytes 1573376 | tf_op jit(solution)/shard_map/scatter | solution.py:125
  527.0 20.6 %copy.117 = bf16[3,96,4096]{1,0,2:T(4,128)(2,1)} copy(bf16[3,96,4096]{1,2,0:T(8,128)(2,1)S(1)} %pad_maximum_fusion.1) | data formatting | bytes 4718592 | tf_op jit(solution)/shard_map/stack | solution.py:133
  555.3 46.1 %all-to-all-done.3 = bf16[3,96,4096]{1,0,2:T(4,128)(2,1)} async-done(((bf16[3,96,4096]{1,0,2:T(4,128)(2,1)}), bf16[3,96,4096]{1,0,2:T(4,128)(2,1)}, u32[]{:S(2)}, u32[]{:S(2)}) %all-to-all-start.3) | async-done | bytes 2359328 | tf_op jit(solution)/shard_map/all_to_all | solution.py:132
  612.9 8.6 %copy.123 = bf16[4,768,768]{2,0,1:T(4,128)(2,1)} copy(bf16[4,768,768]{1,2,0:T(8,128)(2,1)} %pad_maximum_fusion) | data formatting | bytes 9437184 | tf_op jit(solution)/shard_map/stack | solution.py:152
  623.3 84.5 %all-reduce.6.cloned.1.call-done = bf16[4,768,768]{2,0,1:T(4,128)(2,1)} async-done(((bf16[4,768,768]{2,0,1:T(4,128)(2,1)}), bf16[4,768,768]{2,0,1:T(4,128)(2,1)}) %all-reduce.6.cloned.1.call-update) | async-done | bytes 4718608
  710.0 40.3 %all-reduce.4.cloned.1.call-done = bf16[4,96,768]{2,0,1:T(4,128)(2,1)} async-done(((bf16[4,96,768]{2,0,1:T(4,128)(2,1)}), bf16[4,96,768]{2,0,1:T(4,128)(2,1)}) %all-reduce.4.cloned.1.call-update) | async-done | bytes 589840 | tf_op jit(solution)/shard_map/psum | solution.py:163
  757.5 33.5 %all-gather.2.cloned.1.call-done = bf16[4,768,768]{2,0,1:T(4,128)(2,1)} async-done(((bf16[4,96,768]{2,0,1:T(4,128)(2,1)}), bf16[4,768,768]{2,0,1:T(4,128)(2,1)}) %all-gather.2.cloned.1.call-update) | async-done | bytes 4718608 | tf_op jit(solution)/shard_map/all_gather | solution.py:164
  790.9 8.0 convert_multiply_fusion
  799.0 21.6 %fusion.58 = (f32[1,768,768]{2,0,1:T(1,128)S(1)}, f32[1,768,768]{2,0,1:T(1,128)S(1)}, f32[1,768,768]{2,0,1:T(1,128)S(1)}, f32[1,768,768]{2,0,1:T(1,128)S(1)}) fusion(f32[4,768,768]{2,0,1:T(4,128)} %convert_multiply_fusion), kind=kLoop, calls=%fused_computation.113 | loop fusion | bytes 18874368 | tf_op jit(solution)/shard_map/slice | solution.py:169
  (297 shorter events, 268.9 us)
Async XLA Ops:
  7.2 9.3 %copy-start.27 = (bf16[1,512,768]{2,1,0:T(8,128)(2,1)S(1)}, bf16[1,512,768]{2,1,0:T(8,128)(2,1)}, u32[]{:S(2)}) copy-start(bf16[1,512,768]{2,1,0:T(8,128)(2,1)} %param.11) | copy-start | bytes 2359300
  11.3 17.8 %all-to-all-start.1 = ((bf16[8,96,512]{2,1,0:T(8,128)(2,1)}), bf16[8,96,512]{2,1,0:T(8,128)(2,1)S(1)}, u32[]{:S(2)}, u32[]{:S(2)}) async-start(bf16[8,96,512]{2,1,0:T(8,128)(2,1)} %bitcast.40), calls=%async_computation.1 | async-start | bytes 1572864 | tf_op jit(solution)/shard_map/all_to_all | solution.py:44
  24.7 11.6 %copy-start.20 = (s32[1,4096]{1,0:T(1,128)S(1)}, s32[1,4096]{1,0:T(1,128)}, u32[]{:S(2)}) copy-start(s32[1,4096]{1,0:T(1,128)} %param.17) | copy-start | bytes 49156
  29.0 42.6 %all-to-all-start = ((bf16[3,768,512]{2,0,1:T(4,128)(2,1)}), bf16[3,768,512]{2,0,1:T(4,128)(2,1)}, u32[]{:S(2)}, u32[]{:S(2)}) async-start(bf16[3,768,512]{2,0,1:T(4,128)(2,1)} %copy.96), calls=%async_computation | async-start | bytes 6291456 | tf_op jit(solution)/shard_map/all_to_all | solution.py:41
  79.2 30.7 %copy-start.22 = (pred[4096]{0:T(1024)(128)(4,1)S(1)}, pred[4096]{0:T(1024)(128)(4,1)}, u32[]{:S(2)}) copy-start(pred[4096]{0:T(1024)(128)(4,1)} %compare_and_fusion.1) | copy-start | bytes 12292
  171.7 6.5 copy-start.8
  171.7 6.6 copy-start.12
  171.7 6.6 copy-start.14
  195.0 7.2 copy-start.4
  195.0 7.2 copy-start.13
  195.0 7.2 copy-start.15
  245.8 6.5 copy-start.8
  245.8 6.6 copy-start.12
  245.8 6.6 copy-start.14
  269.2 7.2 copy-start.4
  269.2 7.2 copy-start.13
  269.2 7.2 copy-start.15
  320.0 6.6 copy-start.12
  320.0 6.6 copy-start.14
  343.3 7.2 copy-start.4
  343.3 7.2 copy-start.13
  343.3 7.2 copy-start.15
  394.1 6.6 copy-start.12
  394.1 6.6 copy-start.14
  417.5 7.2 copy-start.4
  417.5 7.2 copy-start.13
  417.5 7.2 copy-start.15
  482.0 65.6 %all-to-all-start.2 = ((bf16[96,8,512]{2,0,1:T(8,128)(2,1)}), bf16[96,8,512]{2,0,1:T(8,128)(2,1)}, u32[]{:S(2)}, u32[]{:S(2)}) async-start(bf16[96,8,512]{2,0,1:T(8,128)(2,1)} %copy.110), calls=%async_computation.2 | async-start | bytes 1572864 | tf_op jit(solution)/shard_map/all_to_all | solution.py:131
  547.6 53.8 %all-to-all-start.3 = ((bf16[3,96,4096]{1,0,2:T(4,128)(2,1)}), bf16[3,96,4096]{1,0,2:T(4,128)(2,1)}, u32[]{:S(2)}, u32[]{:S(2)}) async-start(bf16[3,96,4096]{1,0,2:T(4,128)(2,1)} %copy.117), calls=%async_computation.3 | async-start | bytes 8388608 | tf_op jit(solution)/shard_map/all_to_all | solution.py:132
  552.3 155.5 %all-reduce.6.cloned.1.call-start = ((), (), s32[]{:S(2)}) async-start(), calls=%async_computation.6 | async-start | bytes 9437184
  621.5 128.8 %all-reduce.4.cloned.1.call-start = ((), (), s32[]{:S(2)}) async-start(), calls=%async_computation.4 | async-start | bytes 1179648 | tf_op jit(solution)/shard_map/psum | solution.py:163
  709.9 81.0 %all-gather.2.cloned.1.call-start = ((), (), s32[]{:S(2)}) async-start(), calls=%async_computation.5 | async-start | bytes 5308416 | tf_op jit(solution)/shard_map/all_gather | solution.py:164
  (44 other events, 147.9 us)
Sparse Core Ops, SparseCore 0:
  621.6 86.1 all-reduce.5
  710.9 39.3 all-reduce.3
  752.3 38.5 all-gather.1
where the time goes:
time: 844 us; the launch traced here: 834 us
  local copies, waits for them, and re-layouts  265 us (31%)
  waiting for transfers between devices  229 us (27%)
  other arithmetic  181 us (21%)
  matrix products  121 us (14%)
  starting transfers between devices  18.9 us (2%)
  between operations  15.4 us (2%)
    scatter-add x12, other arithmetic, local(): accumulate = jax.vmap(lambda acc, where, vals: acc.at[where].add(vals))  109 us
    unnamed x4, waiting for transfers between devices  84.5 us
    scatter x4, local copies, waits for them, and re-layouts, restore(): return jnp.zeros_like(arr).at[:, order].set(arr)  46.6 us
    all_to_all x1, waiting for transfers between devices, local(): lax.all_to_all(jnp.stack([dq_heads, dk_heads, dv_heads]), 'node', split_a...  46.1 us
    gather x3, local copies, waits for them, and re-layouts, to_blocks(): arr = jnp.take(arr, order, axis=-1)  43.3 us
    psum x1, waiting for transfers between devices, local(): share = lax.psum(share.astype(jnp.bfloat16), 'dp').astype(jnp.float32)  40.3 us
    all_gather x1, waiting for transfers between devices, local(): lax.all_gather(share.astype(jnp.bfloat16), 'node', axis=1, tiled=True)  33.5 us
    dot_general x4, matrix products, step(): jnp.einsum('hdgi,hgmdj->hgimj', up_part, v_got, preferred_element_type=jn...  28.6 us
  transfers between devices with their start and end apart: 7, of which 6 were waited for; matrix products, arithmetic and copies ran while one was open for 11% of the time, Pallas kernels for 0%

commit v1 on v0

v1 whole, which is shorter than its diff:
```python
import functools
import math

import jax
import jax.numpy as jnp
from jax import lax
from jax.experimental import pallas as pl
from jax.experimental.pallas import tpu as pltpu
from jax.sharding import PartitionSpec as P

H = 32
HD = 24
BLOCK = 128
WIDE = 2 * BLOCK
F32 = jnp.float32
BF16 = jnp.bfloat16


def attention_kernel(
    heads, slots, ids_ref, cnt_ref, row_ref, col_ref, a_ref, out_ref, vkt, vkn, rhs, acc, odq, packed
):
    sources, _, chunk = a_ref.shape
    nblocks = vkt.shape[1]
    per_chunk = chunk // BLOCK
    scale = 1.0 / math.sqrt(HD)
    to_exp2 = scale * math.log2(math.e)
    zero = jnp.zeros((HD, BLOCK), F32)

    def reorder(turn, carry):
        row = row_ref[turn]
        place = lax.broadcasted_iota(jnp.int32, (chunk, WIDE), 0)
        total = None
        for s in range(sources):
            onehot = jnp.where(place == row - s * chunk, 1.0, 0.0).astype(BF16)
            part = jnp.dot(a_ref[s], onehot, preferred_element_type=F32)
            total = part if total is None else total + part
        for h in range(heads):
            for half in range(2):
                b = turn * 2 + half
                base = h * 4 * HD
                lanes = slice(half * BLOCK, (half + 1) * BLOCK)
                vk = total[base : base + 2 * HD, lanes]
                up = total[base + 2 * HD : base + 3 * HD, lanes]
                q = total[base + 3 * HD : base + 4 * HD, lanes]
                vkt[h, b] = vk.astype(BF16)
                vkn[h, b] = vk.T.astype(BF16)
                rhs[h, b] = jnp.concatenate(
                    [
                        jnp.concatenate([up, zero], axis=1),
                        jnp.concatenate([zero, q], axis=1),
                    ],
                    axis=0,
                ).astype(BF16)
                acc[h, b] = jnp.zeros((2 * HD, BLOCK), F32)
        return carry

    lax.fori_loop(0, nblocks // 2, reorder, 0)

    def attend(b, carry):
        for h in range(heads):
            first = (h * nblocks + b) * slots
            ids = [ids_ref[first + m] for m in range(slots)]
            count = cnt_ref[h * nblocks + b]
            right = rhs[h, b]
            both = []
            for m in range(slots):
                both.append(jnp.dot(vkn[h, ids[m]], right, preferred_element_type=F32))
            score = [
                jnp.where(m < count, both[m][:, BLOCK:], -1e30) for m in range(slots)
            ]
            top = functools.reduce(
                jnp.maximum, [jnp.max(s, axis=0, keepdims=True) for s in score]
            )
            expo = [jnp.exp2((s - top) * to_exp2) for s in score]
            norm = sum(jnp.sum(e, axis=0, keepdims=True) for e in expo)
            inv = 1.0 / norm
            prob = [e * inv for e in expo]
            grad = [both[m][:, :BLOCK] for m in range(slots)]
            delta = sum(
                jnp.sum(prob[m] * grad[m], axis=0, keepdims=True) for m in range(slots)
            )
            pd = jnp.concatenate(
                [
                    jnp.concatenate(
                        [
                            prob[m].astype(BF16),
                            (prob[m] * (grad[m] - delta) * scale).astype(BF16),
                        ],
                        axis=1,
                    )
                    for m in range(slots)
                ],
                axis=0,
            )
            left = jnp.concatenate([vkt[h, ids[m]] for m in range(slots)], axis=1)
            forward = jnp.dot(left, pd, preferred_element_type=F32)
            odq[h, b] = jnp.concatenate([forward[:HD, :BLOCK], forward[HD:, BLOCK:]], axis=0)
            back = lax.dot_general(
                right, pd, (((1,), (1,)), ((), ())), preferred_element_type=F32
            )
            for m in range(slots):
                acc[h, ids[m]] += back[:, m * BLOCK : (m + 1) * BLOCK]
        return carry

    lax.fori_loop(0, nblocks, attend, 0)

    def pack(g, carry):
        for j in range(per_chunk):
            b = g * per_chunk + j
            pieces = [odq[h, b, :HD] for h in range(heads)]
            pieces += [odq[h, b, HD:] for h in range(heads)]
            pieces += [acc[h, b, :HD] for h in range(heads)]
            pieces += [acc[h, b, HD:] for h in range(heads)]
            packed[g, :, j * BLOCK : (j + 1) * BLOCK] = jnp.concatenate(pieces, axis=0).astype(BF16)
        return carry

    lax.fori_loop(0, sources, pack, 0)

    def restore(s, carry):
        lane = lax.broadcasted_iota(jnp.int32, (chunk, BLOCK), 1)
        for part in range(chunk // WIDE):
            low = lane + (s * chunk + part * WIDE)
            high = low + BLOCK
            total = None
            for g in range(sources):
                col = col_ref[g * chunk : (g + 1) * chunk]
                onehot = jnp.concatenate(
                    [
                        jnp.where(col == low, 1.0, 0.0).astype(BF16),
                        jnp.where(col == high, 1.0, 0.0).astype(BF16),
                    ],
                    axis=1,
                )
                got = jnp.dot(packed[g], onehot, preferred_element_type=F32)
                total = got if total is None else total + got
            out_ref[s, :, part * WIDE : (part + 1) * WIDE] = total.astype(BF16)
        return carry

    lax.fori_loop(0, sources, restore, 0)


def attention(ids, counts, order, arrived, heads):
    sources, rows, chunk = arrived.shape
    total = order.shape[0]
    nblocks = total // BLOCK
    slots = ids.shape[-1]
    vmem = pl.BlockSpec(memory_space=pltpu.VMEM)
    smem = pl.BlockSpec(memory_space=pltpu.SMEM)
    return pl.pallas_call(
        functools.partial(attention_kernel, heads, slots),
        out_shape=jax.ShapeDtypeStruct((sources, rows, chunk), BF16),
        in_specs=[smem, smem, vmem, vmem, vmem],
        out_specs=vmem,
        scratch_shapes=[
            pltpu.VMEM((heads, nblocks, 2 * HD, BLOCK), BF16),
            pltpu.VMEM((heads, nblocks, BLOCK, 2 * HD), BF16),
            pltpu.VMEM((heads, nblocks, 2 * HD, WIDE), BF16),
            pltpu.VMEM((heads, nblocks, 2 * HD, BLOCK), F32),
            pltpu.VMEM((heads, nblocks, 2 * HD, BLOCK), F32),
            pltpu.VMEM((sources, rows, chunk), BF16),
        ],
        compiler_params=pltpu.CompilerParams(vmem_limit_bytes=52 * 1024 * 1024),
        cost_estimate=pl.CostEstimate(
            flops=60_000_000_000, bytes_accessed=100_000_000, transcendentals=0
        ),
        name="attention",
    )(
        ids.reshape(-1),
        counts.reshape(-1),
        order.reshape(total // WIDE, 1, WIDE),
        jnp.broadcast_to(order[:, None], (total, BLOCK)),
        arrived,
    )


def project(weight, rows):
    return lax.dot_general(
        weight, rows, (((0,), (1,)), ((), ())), preferred_element_type=F32
    ).astype(BF16)


def local(
    vertex_embeddings,
    incoming_adjoint,
    asking_projector_matrix,
    lookup_projector_matrix,
    content_projector_matrix,
    final_projector_matrix,
    grouped_vertex_permutation,
    listed_tiles,
    active_tile_tally,
):
    rows = vertex_embeddings[0]
    cotan = incoming_adjoint[0]
    parts = lax.axis_size("node")
    groups = lax.axis_size("dp")
    heads = H // parts
    feats = heads * HD
    chunk, width = rows.shape
    order = grouped_vertex_permutation[0]
    total = order.shape[0]

    pq = project(asking_projector_matrix, rows)
    pk = project(lookup_projector_matrix, rows)
    pv = project(content_projector_matrix, rows)
    up = lax.dot_general(
        final_projector_matrix, cotan, (((1,), (1,)), ((), ())), preferred_element_type=F32
    ).astype(BF16)
    outgoing = jnp.stack(
        [x.reshape(parts, heads, HD, chunk) for x in (pv, pk, up, pq)], axis=2
    ).reshape(parts, 4 * feats, chunk)
    arrived = lax.all_to_all(outgoing, "node", split_axis=0, concat_axis=0, tiled=True)
    all_rows = lax.all_gather(rows, "node", axis=0, tiled=True)
    all_cotan = lax.all_gather(cotan, "node", axis=0, tiled=True)

    first = lax.axis_index("node") * heads
    lists = lax.dynamic_slice_in_dim(listed_tiles[0], first, heads, 0)
    counts = lax.dynamic_slice_in_dim(active_tile_tally[0], first, heads, 0)
    mine = attention(lists, counts, order, arrived, heads)

    got = lax.all_to_all(mine, "node", split_axis=0, concat_axis=0, tiled=True)
    got = got.reshape(parts, 4, feats, chunk)

    by_type = mine.reshape(parts, 4, feats, chunk)
    grads = by_type[:, 1:].transpose(1, 2, 0, 3).reshape(3 * feats, total)
    outs = by_type[:, 0].transpose(1, 0, 2).reshape(feats, total)
    partial = jnp.concatenate(
        [
            jnp.dot(outs, all_cotan, preferred_element_type=F32).astype(BF16),
            jnp.dot(grads, all_rows, preferred_element_type=F32).astype(BF16),
        ],
        axis=0,
    ).reshape(groups, 4 * feats // groups, width)
    shares = lax.all_to_all(partial, "dp", split_axis=0, concat_axis=0, tiled=True)
    share = jnp.sum(shares.astype(F32), axis=0).astype(BF16)
    summed = lax.all_gather(share, ("node", "dp"), axis=0, tiled=True)
    summed = summed.reshape(parts, 4, feats, width)
    factor = 1.0 / math.sqrt(groups * total)

    def whole(which):
        return summed[:, which].reshape(parts * feats, width)

    grad_out = whole(0).astype(F32) * factor
    grad_query = whole(1).T.astype(F32) * factor
    grad_value = whole(2).T.astype(F32) * factor
    grad_key = whole(3).T.astype(F32) * factor

    def nodes(which):
        return got[:, which].reshape(parts * feats, chunk)

    dims_first = (((0,), (0,)), ((), ()))
    dims_back = (((0,), (1,)), ((), ()))
    result = lax.dot_general(
        nodes(0), final_projector_matrix, dims_first, preferred_element_type=F32
    ).astype(BF16)
    backward = (
        lax.dot_general(nodes(1), asking_projector_matrix, dims_back, preferred_element_type=F32)
        + lax.dot_general(nodes(3), lookup_projector_matrix, dims_back, preferred_element_type=F32)
        + lax.dot_general(nodes(2), content_projector_matrix, dims_back, preferred_element_type=F32)
    ).astype(BF16)
    return (result[None], backward[None], grad_query, grad_key, grad_value, grad_out)


def solution(mesh):
    placed = (
        P("dp", "node", None),
        P("dp", "node", None),
        P(),
        P(),
        P(),
        P(),
        P("dp", None),
        P("dp", None, None, None),
        P("dp", None, None),
    )
    return jax.shard_map(
        local,
        mesh=mesh,
        in_specs=placed,
        out_specs=(P("dp", "node", None), P("dp", "node", None), P(), P(), P(), P()),
        check_vma=False,
    )
```

time: 844 us -> 302 us (0.36); the launches traced: 834 us -> 302 us
  local copies, waits for them, and re-layouts: 265 us -> 21.2 us
  other arithmetic: 181 us -> 8.18 us
  waiting for transfers between devices: 229 us -> 70 us
  matrix products: 121 us -> 19.9 us
  Pallas kernels: 0 us -> 98.8 us
  blocking collectives: 0 us -> 64 us
  starting transfers between devices: 18.9 us -> 5.6 us
    scatter-add x12 -> x0, other arithmetic: 109 us -> none  [local(): accumulate = jax.vmap(lambda acc, where, vals: acc.at[where].add(vals))]
    dot_general x32 -> x6, matrix products: 115 us -> 15.3 us  [the longest x1 6.25 us: local(): jnp.dot(grads, all_rows, preferred_element_type=F32).astype(BF16)]
    pallas_call x0 -> x1, Pallas kernels: none -> 98.8 us  [attention(): pl.pallas_call(functools.partial(attention_kernel, heads, slots), out_sha...]
    unnamed x4 -> x3, waiting for transfers between devices: 84.5 us -> 1.39 us
    all_to_all x0 -> x2, blocking collectives: none -> 64 us  [the longest x1 46.7 us: local(): got = lax.all_to_all(mine, 'node', split_axis=0, concat_axis=0, tiled=True)]
    gather x19 -> x0, local copies, waits for them, and re-layouts: 63.9 us -> none  [the longest x3 43.3 us: to_blocks(): arr = jnp.take(arr, order, axis=-1)]
    scatter x4 -> x0, local copies, waits for them, and re-layouts: 46.6 us -> none  [restore(): return jnp.zeros_like(arr).at[:, order].set(arr)]
    psum x1 -> x0, waiting for transfers between devices: 40.3 us -> none  [local(): share = lax.psum(share.astype(jnp.bfloat16), 'dp').astype(jnp.float32)]
  transfers between devices with their start and end apart: 7 -> 4, of which waited for: 6 -> 2; matrix products, arithmetic and copies ran while one was open for 11% -> 10% of each run, Pallas kernels for 0% -> 33%
where the time goes in v1:
time: 302 us
  Pallas kernels  98.8 us (33%)
  waiting for transfers between devices  70 us (23%)
  blocking collectives  64 us (21%)
  local copies, waits for them, and re-layouts  21.2 us (7%)
  matrix products  19.9 us (7%)
  between operations  13.9 us (5%)
  other arithmetic  8.18 us (3%)
  starting transfers between devices  5.6 us (2%)
    pallas_call x1, Pallas kernels, attention(): pl.pallas_call(functools.partial(attention_kernel, heads, slots), out_sha...  98.8 us
    all_to_all x1, waiting for transfers between devices, local(): lax.all_to_all(outgoing, 'node', split_axis=0, concat_axis=0, tiled=True)  53.8 us
    all_to_all x1, blocking collectives, local(): got = lax.all_to_all(mine, 'node', split_axis=0, concat_axis=0, tiled=True)  46.7 us
    all_to_all x1, blocking collectives, local(): lax.all_to_all(partial, 'dp', split_axis=0, concat_axis=0, tiled=True)  17.3 us
    all_gather x1, waiting for transfers between devices, local(): summed = lax.all_gather(share, ('node', 'dp'), axis=0, tiled=True)  14.8 us
    unnamed x25, local copies, waits for them, and re-layouts  14.4 us
    dot_general x1, matrix products, local(): jnp.dot(grads, all_rows, preferred_element_type=F32).astype(BF16)  6.25 us
  transfers between devices with their start and end apart: 4, of which 2 were waited for; matrix products, arithmetic and copies ran while one was open for 10% of the time, Pallas kernels for 33%

profile of v1, /device:TPU:0, one launch (start us, length us, event | category | flops | bytes accessed | tf_op | source)
XLA Modules:
  0.0 301.6 jit_solution(1734609706799569097)
XLA Ops:
  7.2 0.7 all-gather.10.cloned.1.call-update
  8.0 0.7 all-gather.8.cloned.1.call-update
  8.7 2.2 convolution_convert_fusion.1
  10.9 0.8 convolution_convert_fusion.2
  11.7 0.5 copy-done.7
  12.2 0.8 convolution_convert_fusion.3
  13.4 0.8 convolution_convert_fusion.4
  14.3 1.9 pad_maximum_fusion
  16.1 5.3 %all-to-all-start = ((bf16[8,384,512]{2,1,0:T(8,128)(2,1)}), bf16[8,384,512]{2,1,0:T(8,128)(2,1)}, u32[]{:S(2)}, u32[]{:S(2)}) async-start(bf16[8,384,512]{2,1,0:T(8,128)(2,1)} %bitcast.88), calls=%async_computation | async-start | bytes 6291456 | tf_op jit(solution)/shard_map/all_to_all | solution.py:212
  21.7 0.7 constant_dynamic-slice_fusion.1
  22.6 0.7 constant_dynamic-slice_fusion
  23.4 53.8 %all-to-all-done.a_ref = bf16[8,384,512]{2,1,0:T(8,128)(2,1)} async-done(((bf16[8,384,512]{2,1,0:T(8,128)(2,1)}), bf16[8,384,512]{2,1,0:T(8,128)(2,1)}, u32[]{:S(2)}, u32[]{:S(2)}) %all-to-all-start) | async-done | bytes 3145760 | tf_op jit(solution)/shard_map/all_to_all | solution.py:212
  77.1 2.9 broadcast_in_dim.14.col_ref
  80.0 98.8 %attention.1 = bf16[8,384,512]{2,1,0:T(8,128)(2,1)} custom-call(s32[512]{0:T(512)S(1)} %reshape.56.ids_ref, s32[128]{0:T(128)S(1)} %reshape.57.cnt_ref, s32[16,1,256]{2,1,0:T(1,128)S(1)} %bitcast.85, s32[4096,128]{1,0:T(8,128)} %broadcast_in_dim.14.col_ref, bf16[8,384,512]{2,1,0:T(8,128)(2,1)} %all-to-all-done.a_ref), custom_call_target="tpu_custom_call" | custom-call | flops 60000002048 | bytes 100000000 | tf_op jit(solution)/shard_map/attention/pallas_call | solution.py:149
  178.8 1.8 slice.45
  180.6 1.3 copy.33
  181.9 2.5 copy.35
  184.4 1.2 slice_bitcast_fusion
  185.7 6.3 %fusion.6 = bf16[288,768]{1,0:T(8,128)(2,1)} fusion(bf16[288,4096]{1,0:T(8,128)(2,1)} %bitcast.98, bf16[1,4096,768]{2,1,0:T(8,128)(2,1)} %all-gather.10.cloned.1.call-done), kind=kOutput, calls=%fused_computation.17 | convolution fusion | flops 1812160512 | bytes 9093120 | tf_op jit(solution)/shard_map/dot_general | solution.py:230
  192.0 4.0 %fusion.9 = bf16[96,768]{1,0:T(8,128)(2,1)S(1)} fusion(bf16[96,4096]{1,0:T(8,128)(2,1)S(1)} %bitcast.95, bf16[1,4096,768]{2,1,0:T(8,128)(2,1)} %all-gather.8.cloned.1.call-done), kind=kOutput, calls=%fused_computation.18 | convolution fusion | flops 604053504 | bytes 7225344 | tf_op jit(solution)/shard_map/dot_general | solution.py:229
  196.0 17.3 %all_to_all.15 = bf16[4,96,768]{2,1,0:T(8,128)(2,1)S(1)} all-to-all(bf16[4,96,768]{2,1,0:T(8,128)(2,1)S(1)} %bitcast.99), channel_id=1, replica_groups=mesh['dp'=4,'node'=8] {'dp'}, dimensions={0} | all-to-all | bytes 1179648 | tf_op jit(solution)/shard_map/all_to_all | solution.py:234
  213.3 0.8 reduce_sum.12
  214.1 46.7 %all_to_all.16 = bf16[8,384,512]{2,1,0:T(8,128)(2,1)S(1)} all-to-all(bf16[8,384,512]{2,1,0:T(8,128)(2,1)} %attention.1), channel_id=1, replica_groups=mesh['dp'=4,'node'=8] {'node'}, dimensions={0} | all-to-all | bytes 6291456 | tf_op jit(solution)/shard_map/all_to_all | solution.py:221
  261.1 1.7 fusion.4
  262.8 0.8 fusion.17
  264.1 0.8 fusion.18
  264.9 1.7 fusion.5
  266.7 14.8 %all-gather.6.cloned.1.call-done = bf16[3072,768]{1,0:T(8,128)(2,1)} async-done(((bf16[96,768]{1,0:T(8,128)(2,1)}), bf16[3072,768]{1,0:T(8,128)(2,1)}) %all-gather.6.cloned.1.call-update) | async-done | bytes 4718608 | tf_op jit(solution)/shard_map/all_gather | solution.py:236
  281.5 5.5 %convert_multiply_fusion = (f32[8,1,96,768]{3,2,1,0:T(8,128)}, f32[8,1,96,768]{3,2,1,0:T(8,128)S(1)}, f32[8,1,96,768]{3,2,1,0:T(8,128)}, f32[8,1,96,768]{3,2,1,0:T(8,128)}) fusion(bf16[8,4,96,768]{3,2,1,0:T(8,128)(2,1)} %bitcast.94), kind=kLoop, calls=%fused_computation.5 | loop fusion | flops 4718592 | bytes 14155776 | tf_op jit(solution)/shard_map/mul | solution.py:243
  287.0 3.0 %copy.29 = f32[768,768]{1,0:T(8,128)} copy(f32[768,768]{0,1:T(8,128)} %bitcast.92) | data formatting | bytes 4718592
  290.0 3.0 %copy.30 = f32[768,768]{1,0:T(8,128)} copy(f32[768,768]{0,1:T(8,128)} %bitcast.91) | data formatting | bytes 4718592
  293.1 1.9 copy.31
  (29 shorter events, 2.0 us)
Async XLA Ops:
  7.2 3.7 %copy-start = (bf16[768,768]{1,0:T(8,128)(2,1)S(1)}, bf16[768,768]{1,0:T(8,128)(2,1)}, u32[]{:S(2)}) copy-start(bf16[768,768]{1,0:T(8,128)(2,1)} %param.14) | copy-start | bytes 3538948
  7.2 1.5 copy-start.3
  7.2 178.5 %all-gather.10.cloned.1.call-start = ((), (), s32[]{:S(2)}) async-start(), calls=%async_computation.5 | async-start | bytes 7077888 | tf_op jit(solution)/shard_map/all_gather | solution.py:213
  7.9 184.0 %all-gather.8.cloned.1.call-start = ((), (), s32[]{:S(2)}) async-start(), calls=%async_computation.4 | async-start | bytes 7077888 | tf_op jit(solution)/shard_map/all_gather | solution.py:214
  8.7 2.2 copy-start.4
  10.9 1.3 copy-start.7
  12.2 1.3 copy-start.2
  16.1 61.0 %copy-start.1 = (s32[1,4096]{1,0:T(1,128)S(1)}, s32[1,4096]{1,0:T(1,128)}, u32[]{:S(2)}) copy-start(s32[1,4096]{1,0:T(1,128)} %param.15) | copy-start | bytes 49156
  16.1 61.0 %all-to-all-start = ((bf16[8,384,512]{2,1,0:T(8,128)(2,1)}), bf16[8,384,512]{2,1,0:T(8,128)(2,1)}, u32[]{:S(2)}, u32[]{:S(2)}) async-start(bf16[8,384,512]{2,1,0:T(8,128)(2,1)} %bitcast.88), calls=%async_computation | async-start | bytes 6291456 | tf_op jit(solution)/shard_map/all_to_all | solution.py:212
  21.4 260.1 %all-gather.6.cloned.1.call-start = ((), (), s32[]{:S(2)}) async-start(), calls=%async_computation.3 | async-start | bytes 4866048 | tf_op jit(solution)/shard_map/all_gather | solution.py:236
  192.0 4.0 %copy-start.5 = (bf16[288,768]{1,0:T(8,128)(2,1)S(1)}, bf16[288,768]{1,0:T(8,128)(2,1)}, u32[]{:S(2)}) copy-start(bf16[288,768]{1,0:T(8,128)(2,1)} %fusion.6) | copy-start | bytes 1327108
  261.1 1.7 copy-start.6
  262.8 1.3 copy-start.8
Sparse Core Ops, SparseCore 0:
  9.9 74.2 all-gather.9
  86.1 45.5 all-gather.7
  214.2 67.2 all-gather.5

commit v2 on v1

--- a/solution.py
+++ b/solution.py
@@ -210,8 +210,9 @@
         [x.reshape(parts, heads, HD, chunk) for x in (pv, pk, up, pq)], axis=2
     ).reshape(parts, 4 * feats, chunk)
     arrived = lax.all_to_all(outgoing, "node", split_axis=0, concat_axis=0, tiled=True)
-    all_rows = lax.all_gather(rows, "node", axis=0, tiled=True)
-    all_cotan = lax.all_gather(cotan, "node", axis=0, tiled=True)
+    arrived, late_rows, late_cotan = lax.optimization_barrier((arrived, rows, cotan))
+    all_rows = lax.all_gather(late_rows, "node", axis=0, tiled=True)
+    all_cotan = lax.all_gather(late_cotan, "node", axis=0, tiled=True)
 
     first = lax.axis_index("node") * heads
     lists = lax.dynamic_slice_in_dim(listed_tiles[0], first, heads, 0)

time: 302 us -> 286 us (0.947)
  waiting for transfers between devices: 70 us -> 14.6 us
  blocking collectives: 64 us -> 109 us
  starting transfers between devices: 5.6 us -> 0.3 us
    all_to_all x1 -> x0, waiting for transfers between devices: 53.8 us -> none  [local(): lax.all_to_all(outgoing, 'node', split_axis=0, concat_axis=0, tiled=True)]
    all_to_all x0 -> x1, blocking collectives: none -> 42.9 us  [local(): lax.all_to_all(outgoing, 'node', split_axis=0, concat_axis=0, tiled=True)]
    all_to_all x1 -> x0, starting transfers between devices: 5.3 us -> none  [local(): lax.all_to_all(outgoing, 'node', split_axis=0, concat_axis=0, tiled=True)]
  transfers between devices with their start and end apart: 4 -> 3, of which waited for: 2 -> 1; matrix products, arithmetic and copies ran while one was open for 10% -> 8% of each run, Pallas kernels for 33% -> 35%
where the time goes in v2:
time: 286 us; the launch traced here: 285 us
  blocking collectives  109 us (38%)
  Pallas kernels  99.2 us (35%)
  local copies, waits for them, and re-layouts  21 us (7%)
  matrix products  20.2 us (7%)
  waiting for transfers between devices  14.6 us (5%)
  between operations  13.9 us (5%)
  other arithmetic  6.75 us (2%)
    pallas_call x1, Pallas kernels, attention(): pl.pallas_call(functools.partial(attention_kernel, heads, slots), out_sha...  99.2 us
    all_to_all x1, blocking collectives, local(): got = lax.all_to_all(mine, 'node', split_axis=0, concat_axis=0, tiled=True)  46.7 us
    all_to_all x1, blocking collectives, local(): lax.all_to_all(outgoing, 'node', split_axis=0, concat_axis=0, tiled=True)  42.9 us
    all_to_all x1, blocking collectives, local(): lax.all_to_all(partial, 'dp', split_axis=0, concat_axis=0, tiled=True)  19.8 us
    unnamed x25, local copies, waits for them, and re-layouts  14.3 us
    all_gather x1, waiting for transfers between devices, local(): summed = lax.all_gather(share, ('node', 'dp'), axis=0, tiled=True)  13.9 us
    dot_general x1, matrix products, local(): jnp.dot(grads, all_rows, preferred_element_type=F32).astype(BF16)  6.25 us
  transfers between devices with their start and end apart: 3, of which 1 were waited for; matrix products, arithmetic and copies ran while one was open for 8% of the time, Pallas kernels for 35%

profile of v2, /device:TPU:0, one launch (start us, length us, event | category | flops | bytes accessed | tf_op | source)
XLA Modules:
  0.0 285.4 jit_solution(81356101522122033)
XLA Ops:
  7.2 2.5 convolution_convert_fusion.1
  9.8 0.8 convolution_convert_fusion.3
  10.6 0.4 copy-done.2
  11.0 0.8 convolution_convert_fusion.4
  12.1 0.8 convolution_convert_fusion.2
  13.0 0.4 pad_maximum_fusion
  13.4 42.9 %all_to_all.15.a_ref = bf16[8,384,512]{2,1,0:T(8,128)(2,1)} all-to-all(bf16[8,384,512]{2,1,0:T(8,128)(2,1)S(1)} %bitcast.81), channel_id=1, replica_groups=mesh['dp'=4,'node'=8] {'node'}, dimensions={0} | all-to-all | bytes 6291456 | tf_op jit(solution)/shard_map/all_to_all | solution.py:212
  56.4 0.7 all-gather.4.cloned.1.call-update
  57.3 0.7 constant_dynamic-slice_fusion.1
  58.2 0.7 constant_dynamic-slice_fusion
  59.0 2.9 %broadcast_in_dim.14.col_ref = s32[4096,128]{1,0:T(8,128)} broadcast(s32[4096]{0:T(1024)S(1)} %bitcast.76), dimensions={0} | broadcast | bytes 2113536 | tf_op jit(solution)/shard_map/broadcast_in_dim | solution.py:171
  61.9 99.2 %attention.1 = bf16[8,384,512]{2,1,0:T(8,128)(2,1)} custom-call(s32[512]{0:T(512)S(1)} %reshape.56.ids_ref, s32[128]{0:T(128)S(1)} %reshape.57.cnt_ref, s32[16,1,256]{2,1,0:T(1,128)S(1)} %bitcast.77, s32[4096,128]{1,0:T(8,128)} %broadcast_in_dim.14.col_ref, bf16[8,384,512]{2,1,0:T(8,128)(2,1)} %all_to_all.15.a_ref), custom_call_target="tpu_custom_call" | custom-call | flops 60000002048 | bytes 100000000 | tf_op jit(solution)/shard_map/attention/pallas_call | solution.py:149
  161.2 1.8 slice.45
  163.0 1.3 copy.33
  164.3 2.5 copy.35
  166.8 1.2 slice_bitcast_fusion
  168.1 6.3 %convolution_convert_fusion.5 = bf16[288,768]{1,0:T(8,128)(2,1)} fusion(bf16[288,4096]{1,0:T(8,128)(2,1)} %bitcast.90, bf16[4096,768]{1,0:T(8,128)(2,1)} %all-gather.6.cloned.1.call-done), kind=kOutput, calls=%fused_computation.13 | convolution fusion | flops 1812160512 | bytes 9093120 | tf_op jit(solution)/shard_map/dot_general | solution.py:231
  174.3 4.0 %convolution_convert_fusion.6 = bf16[96,768]{1,0:T(8,128)(2,1)S(1)} fusion(bf16[96,4096]{1,0:T(8,128)(2,1)S(1)} %bitcast.87, bf16[4096,768]{1,0:T(8,128)(2,1)} %all-gather.4.cloned.1.call-done), kind=kOutput, calls=%fused_computation.14 | convolution fusion | flops 604053504 | bytes 7225344 | tf_op jit(solution)/shard_map/dot_general | solution.py:230
  178.3 19.8 %all_to_all.16 = bf16[4,96,768]{2,1,0:T(8,128)(2,1)S(1)} all-to-all(bf16[4,96,768]{2,1,0:T(8,128)(2,1)S(1)} %bitcast.91), channel_id=1, replica_groups=mesh['dp'=4,'node'=8] {'dp'}, dimensions={0} | all-to-all | bytes 1179648 | tf_op jit(solution)/shard_map/all_to_all | solution.py:235
  198.1 0.8 reduce_sum.12
  198.9 46.7 %all_to_all.17 = bf16[8,384,512]{2,1,0:T(8,128)(2,1)S(1)} all-to-all(bf16[8,384,512]{2,1,0:T(8,128)(2,1)} %attention.1), channel_id=1, replica_groups=mesh['dp'=4,'node'=8] {'node'}, dimensions={0} | all-to-all | bytes 6291456 | tf_op jit(solution)/shard_map/all_to_all | solution.py:222
  245.6 0.3 fusion.6
  245.9 1.7 fusion
  247.6 0.8 fusion.7
  248.5 0.4 copy-done.8
  248.9 0.8 fusion.8
  249.7 1.7 fusion.1
  251.5 13.9 %all-gather.8.cloned.1.call-done = bf16[3072,768]{1,0:T(8,128)(2,1)} async-done(((bf16[96,768]{1,0:T(8,128)(2,1)}), bf16[3072,768]{1,0:T(8,128)(2,1)}) %all-gather.8.cloned.1.call-update) | async-done | bytes 4718608 | tf_op jit(solution)/shard_map/all_gather | solution.py:237
  265.3 5.5 %convert_multiply_fusion = (f32[8,1,96,768]{3,2,1,0:T(8,128)}, f32[8,1,96,768]{3,2,1,0:T(8,128)S(1)}, f32[8,1,96,768]{3,2,1,0:T(8,128)}, f32[8,1,96,768]{3,2,1,0:T(8,128)}) fusion(bf16[8,4,96,768]{3,2,1,0:T(8,128)(2,1)} %bitcast.86), kind=kLoop, calls=%fused_computation.1 | loop fusion | flops 4718592 | bytes 14155776 | tf_op jit(solution)/shard_map/mul | solution.py:244
  270.8 3.0 %copy.29 = f32[768,768]{1,0:T(8,128)} copy(f32[768,768]{0,1:T(8,128)} %bitcast.84) | data formatting | bytes 4718592
  273.9 3.0 %copy.30 = f32[768,768]{1,0:T(8,128)} copy(f32[768,768]{0,1:T(8,128)} %bitcast.83) | data formatting | bytes 4718592
  276.9 1.9 copy.31
  (28 shorter events, 1.1 us)
Async XLA Ops:
  7.2 4.7 %copy-start = (bf16[768,768]{1,0:T(8,128)(2,1)S(1)}, bf16[768,768]{1,0:T(8,128)(2,1)}, u32[]{:S(2)}) copy-start(bf16[768,768]{1,0:T(8,128)(2,1)} %param.14) | copy-start | bytes 3538948
  7.2 2.5 copy-start.3
  7.2 160.9 %all-gather.6.cloned.1.call-start = ((), (), s32[]{:S(2)}) async-start(), calls=%async_computation.4 | async-start | bytes 7077888 | tf_op jit(solution)/shard_map/all_gather | solution.py:214
  7.2 2.5 copy-start.7
  9.7 1.3 copy-start.2
  11.0 1.1 copy-start.4
  56.3 2.7 copy-start.1
  56.3 118.0 %all-gather.4.cloned.1.call-start = ((), (), s32[]{:S(2)}) async-start(), calls=%async_computation.3 | async-start | bytes 7077888 | tf_op jit(solution)/shard_map/all_gather | solution.py:215
  57.1 208.2 %all-gather.8.cloned.1.call-start = ((), (), s32[]{:S(2)}) async-start(), calls=%async_computation.5 | async-start | bytes 4866048 | tf_op jit(solution)/shard_map/all_gather | solution.py:237
  174.3 4.0 %copy-start.5 = (bf16[288,768]{1,0:T(8,128)(2,1)S(1)}, bf16[288,768]{1,0:T(8,128)(2,1)}, u32[]{:S(2)}) copy-start(bf16[288,768]{1,0:T(8,128)(2,1)} %convolution_convert_fusion.5) | copy-start | bytes 1327108
  245.9 1.7 copy-start.6
  247.6 1.3 copy-start.8
Sparse Core Ops, SparseCore 0:
  56.5 44.9 all-gather.5
  103.3 45.5 all-gather.3
  199.0 66.2 all-gather.7
